TPU v7x, 128 devices: a whole 4x4x4 slice. The times are simulated.
128 devices in a mesh: gx: 8 (over y, core), gy: 16 (over z, x).
Axes of the slice: x: 4, y: 4, z: 4, core: 2. Of those that a mesh axis runs over, the one named last changes fastest.
Arguments:
- ensemble: float32 [128, 524288], P(('gx', 'gy'))
- obs_owner: int32 [2, 2048], replicated, may hold values from 0 to 127, as said below
- obs_local: int32 [2, 2048], replicated, may hold values from 0 to 4095
- obs_value: float32 [2, 2048], replicated, may hold values from -8 to 8
- obs_errvar: float32 [2, 2048], replicated, may hold values from 0.3 to 3
- tile_list: int32 [2, 2048, 8], replicated, may hold values from -1 to 4095, as said below
- weight_index: int32 [2, 2048, 8], replicated, may hold values from 0 to 15
- weight_table: float32 [16], replicated, may hold values from 0.2 to 1
Outputs:
- analysis: float32 [128, 524288], P(('gx', 'gy'))
Inputs may be any that keep to these rules, and one draw needn't show every extreme that they name: `obs_owner`: skewed toward low slabs; the first observation of each batch lies in the last slab, the second in slab 0. `tile_list`: each entry is -1 or a tile within 64 tiles of the observation's own tile, except that the second entry of each batch's first observation is the tile 4096 // 2 tiles away, counted round; tiles may repeat.
All inputs are finite; a program needn't handle non-finite values.
Results may differ from a plain program's by a relative error of at most 0.0003.
Values sent between devices are 32-bit elements; how exact they have to be, the bound alone decides.
No kernel may reach another device: no remote copies, remote signals or barrier semaphores. Data moves between devices by JAX's collectives and lax.ppermute only.
A program may use at most 128 MiB of HBM per device.

v0:
```python
import jax
import jax.numpy as jnp
from jax import lax
from jax.sharding import PartitionSpec as P

TILE = 128
VAR_DEV = 4096


epsilon = 1e-06


def table_lookup(index_row, weight_table):
    table_ids = jnp.arange(weight_table.shape[0], dtype=jnp.int32)
    return jnp.sum(
        (index_row[:, :, None] == table_ids[None, None, :]).astype(jnp.float32)
        * weight_table[None, None, :],
        axis=2,
    )


def weights_for(tiles_row, index_row, weight_table, first_tile, count):
    tile_ids = first_tile + jnp.arange(count, dtype=jnp.int32)
    tile_hit = (tiles_row[:, :, None] == tile_ids[None, None, :]).astype(jnp.float32)
    table_pick = table_lookup(index_row, weight_table)
    return jnp.sum(tile_hit * table_pick[:, :, None], axis=1)


def increments(priors, value_row, errvar_row):
    members = priors.shape[0]
    obs_mean = jnp.mean(priors, axis=0)
    obs_dev = priors - obs_mean
    obs_spread = jnp.sum(obs_dev * obs_dev, axis=0) / (members - 1.0)
    denominator = obs_spread + errvar_row
    post_mean = (errvar_row * obs_mean + obs_spread * value_row) / denominator
    obs_shift = post_mean - obs_mean + (jnp.sqrt(errvar_row / denominator) - 1.0) * obs_dev
    return (obs_dev, obs_spread, obs_shift)


def analyse(slab, obs_dev, obs_spread, obs_shift, weights):
    members, width = slab.shape
    count_obs = obs_dev.shape[1]
    block_obs = min(512, count_obs)
    tiles_here = weights.shape[1]
    state_mean = jnp.mean(slab, axis=0)
    state_dev = slab - state_mean
    total = jnp.zeros_like(slab)
    for start in range(0, count_obs, block_obs):
        dev_part = obs_dev[:, start : start + block_obs]
        covariance = jnp.dot(
            dev_part.T,
            state_dev,
            precision=lax.Precision.HIGHEST,
            preferred_element_type=jnp.float32,
        ) / (members - 1.0)
        regress = covariance / (obs_spread[start : start + block_obs] + epsilon)[:, None]
        localized = (
            regress.reshape(block_obs, tiles_here, width // tiles_here)
            * weights[start : start + block_obs, :, None]
        ).reshape(block_obs, width)
        total = total + jnp.dot(
            obs_shift[:, start : start + block_obs],
            localized,
            precision=lax.Precision.HIGHEST,
            preferred_element_type=jnp.float32,
        )
    return slab + total


def body(
    ensemble, obs_owner, obs_local, obs_value, obs_errvar, tile_list, weight_index, weight_table
):
    count_gy = lax.axis_size("gy")
    my_index = lax.axis_index("gx") * count_gy + lax.axis_index("gy")
    tiles_slab = VAR_DEV // TILE
    batches = obs_owner.shape[0]
    early_list = []
    slabs = lax.all_to_all(ensemble, ("gx", "gy"), split_axis=1, concat_axis=0, tiled=True)
    for batch in range(batches):
        owned = (obs_owner[batch] == my_index).astype(jnp.float32)
        local_rows = jnp.take(slabs, obs_local[batch], axis=1) * owned[None, :]
        priors = lax.psum(local_rows, ("gx", "gy"))
        obs_dev, obs_spread, obs_shift = increments(priors, obs_value[batch], obs_errvar[batch])
        weights = weights_for(
            tile_list[batch], weight_index[batch], weight_table, my_index * tiles_slab, tiles_slab
        )
        slabs = analyse(slabs, obs_dev, obs_spread, obs_shift, weights)
    result = lax.all_to_all(slabs, ("gx", "gy"), split_axis=0, concat_axis=1, tiled=True)
    return result


def solution(mesh):
    placed = (P(("gx", "gy"), None), P(), P(), P(), P(), P(), P(), P())
    return jax.shard_map(
        body, mesh=mesh, in_specs=placed, out_specs=P(("gx", "gy"), None), check_vma=False
    )
```

profile of v0, /device:TPU:1, one launch (start us, length us, event | category | flops | bytes accessed | tf_op | source)
XLA Modules:
  0.0 611.2 jit_solution(2556157694777328442)
XLA Ops:
  6.5 11.5 %all-to-all-start = ((f32[1,128,4096]{2,0,1:T(1,128)}), f32[1,128,4096]{2,0,1:T(1,128)S(1)}, u32[]{:S(2)}, u32[]{:S(2)}) async-start(f32[1,128,4096]{2,0,1:T(1,128)} %bitcast.98), calls=%async_computation | async-start | bytes 4194304 | tf_op jit(solution)/shard_map/all_to_all | solution.py:78
  25.7 21.9 %all-to-all-done = f32[1,128,4096]{2,0,1:T(1,128)S(1)} async-done(((f32[1,128,4096]{2,0,1:T(1,128)}), f32[1,128,4096]{2,0,1:T(1,128)S(1)}, u32[]{:S(2)}, u32[]{:S(2)}) %all-to-all-start) | async-done | bytes 2097184 | tf_op jit(solution)/shard_map/all_to_all | solution.py:78
  47.5 3.8 copy.34
  51.3 8.0 %gather_fusion = f32[2048,128]{1,0:T(8,128)S(1)} fusion(f32[128,4096]{0,1:T(8,128)} %bitcast.88, s32[2048]{0:T(1024)} %fusion.93), kind=kCustom, calls=%fused_computation.clone | custom fusion | bytes 2105344 | tf_op jit(solution)/shard_map/jit(_take)/gather | solution.py:81
  66.0 139.5 %all-reduce.3.cloned.1.call-done = f32[128,2048]{0,1:T(8,128)} async-done(((f32[128,2048]{0,1:T(8,128)}), f32[128,2048]{0,1:T(8,128)}) %all-reduce.3.cloned.1.call-update) | async-done | bytes 1048592 | tf_op jit(solution)/shard_map/psum | solution.py:82
  210.4 7.5 %fusion.67 = f32[512,4096]{1,0:T(8,128)S(1)} fusion(f32[1,128,4096]{2,0,1:T(1,128)S(1)} %all-to-all-done, f32[4096]{0:T(1024)S(1)} %broadcast_multiply_fusion.1, f32[128,2048]{0,1:T(8,128)S(1)} %get-tuple-element.13), kind=kOutput, calls=%fused_computation.80 | convolution fusion | flops 3221749760 | bytes 10764288 | tf_op jit(solution)/shard_map/dot_general | solution.py:50
  217.9 2.5 mul.212
  220.4 11.4 %fusion.12 = f32[128,4096]{1,0:T(8,128)} fusion(f32[64,8,32,128]{3,2,1,0:T(8,128)S(1)} %bitcast.95, f32[512,4096]{1,0:T(8,128)S(1)} %fusion.67, f32[512]{0:T(512)S(1)} %get-tuple-element.40, f32[128,2048]{0,1:T(8,128)S(1)} %multiply_add_fusion.1), kind=kOutput, calls=%fused_computation.21 | convolution fusion | flops 3227516928 | bytes 19138560 | tf_op jit(solution)/shard_map/dot_general | solution.py:61
  231.7 7.7 %fusion.68 = f32[512,4096]{1,0:T(8,128)S(1)} fusion(f32[1,128,4096]{2,0,1:T(1,128)S(1)} %all-to-all-done, f32[4096]{0:T(1024)S(1)} %broadcast_multiply_fusion.1, f32[128,2048]{0,1:T(8,128)S(1)} %get-tuple-element.13), kind=kOutput, calls=%fused_computation.81 | convolution fusion | flops 3221749760 | bytes 10764288 | tf_op jit(solution)/shard_map/dot_general | solution.py:50
  239.5 2.3 mul.209
  241.8 11.6 %fusion.32 = f32[128,4096]{1,0:T(8,128)S(1)} fusion(f32[128,4096]{1,0:T(8,128)} %fusion.12, f32[64,8,32,128]{3,2,1,0:T(8,128)S(1)} %bitcast.91, f32[512,4096]{1,0:T(8,128)S(1)} %fusion.68, f32[512]{0:T(512)S(1)} %get-tuple-element.41, f32[128,2048]{0,1:T(8,128)S(1)} %multiply_add_fusion.1), kind=kOutput, calls=%fused_computation.42 | convolution fusion | flops 3228041216 | bytes 21235712 | tf_op jit(solution)/shard_map/dot_general | solution.py:61
  253.4 7.5 %fusion.66 = f32[512,4096]{1,0:T(8,128)S(1)} fusion(f32[1,128,4096]{2,0,1:T(1,128)S(1)} %all-to-all-done, f32[4096]{0:T(1024)S(1)} %broadcast_multiply_fusion.1, f32[128,2048]{0,1:T(8,128)S(1)} %get-tuple-element.13), kind=kOutput, calls=%fused_computation.79 | convolution fusion | flops 3221749760 | bytes 10764288 | tf_op jit(solution)/shard_map/dot_general | solution.py:50
  260.9 3.5 mul.215
  264.4 11.4 %fusion.33 = f32[128,4096]{1,0:T(8,128)} fusion(f32[128,4096]{1,0:T(8,128)S(1)} %fusion.32, f32[64,8,32,128]{3,2,1,0:T(8,128)S(1)} %bitcast.92, f32[512,4096]{1,0:T(8,128)S(1)} %fusion.66, f32[512]{0:T(512)S(1)} %get-tuple-element.39, f32[128,2048]{0,1:T(8,128)S(1)} %multiply_add_fusion.1), kind=kOutput, calls=%fused_computation.43 | convolution fusion | flops 3228041216 | bytes 21235712 | tf_op jit(solution)/shard_map/dot_general | solution.py:61
  275.8 7.9 %fusion.65 = f32[512,4096]{1,0:T(8,128)S(1)} fusion(f32[1,128,4096]{2,0,1:T(1,128)S(1)} %all-to-all-done, f32[4096]{0:T(1024)S(1)} %broadcast_multiply_fusion.1, f32[128,2048]{0,1:T(8,128)S(1)} %get-tuple-element.13), kind=kOutput, calls=%fused_computation.78 | convolution fusion | flops 3221749760 | bytes 10764288 | tf_op jit(solution)/shard_map/dot_general | solution.py:50
  283.7 2.3 mul.218
  286.0 16.6 %fusion.106 = (f32[4096]{0:T(1024)S(1)}, f32[128,4096]{1,0:T(8,128)}) fusion(f32[128,4096]{1,0:T(8,128)} %fusion.33, f32[64,8,32,128]{3,2,1,0:T(8,128)S(1)} %bitcast.89, f32[512,4096]{1,0:T(8,128)S(1)} %fusion.65, f32[512]{0:T(512)S(1)} %get-tuple-element.38, f32[128,2048]{0,1:T(8,128)S(1)} %multiply_add_fusion.1, f32[1,128,4096]{2,0,1:T(1,128)S(1)} %all-to-all-done), kind=kOutput, calls=%fused_computation.160 | convolution fusion | flops 3229085696 | bytes 23349248 | tf_op jit(solution)/shard_map/dot_general | solution.py:61
  304.6 5.5 gather_fusion.1
  312.1 145.5 %all-reduce.5.cloned.1.call-done = f32[128,2048]{0,1:T(8,128)} async-done(((f32[128,2048]{0,1:T(8,128)}), f32[128,2048]{0,1:T(8,128)}) %all-reduce.5.cloned.1.call-update) | async-done | bytes 1048592 | tf_op jit(solution)/shard_map/psum | solution.py:82
  461.1 9.0 %fusion.61 = f32[512,4096]{1,0:T(8,128)} fusion(f32[128,4096]{1,0:T(8,128)S(1)} %copy-done, f32[4096]{0:T(1024)S(1)} %broadcast_multiply_fusion, f32[128,2048]{0,1:T(8,128)S(1)} %get-tuple-element.11), kind=kOutput, calls=%fused_computation.74 | convolution fusion | flops 3221749760 | bytes 10764288 | tf_op jit(solution)/shard_map/dot_general | solution.py:50
  470.1 9.1 %fusion.63 = f32[512,4096]{1,0:T(8,128)} fusion(f32[128,4096]{1,0:T(8,128)S(1)} %copy-done, f32[4096]{0:T(1024)S(1)} %broadcast_multiply_fusion, f32[128,2048]{0,1:T(8,128)S(1)} %get-tuple-element.11), kind=kOutput, calls=%fused_computation.76 | convolution fusion | flops 3221749760 | bytes 10764288 | tf_op jit(solution)/shard_map/dot_general | solution.py:50
  479.3 7.0 %fusion.59 = f32[512,4096]{1,0:T(8,128)S(1)} fusion(f32[128,4096]{1,0:T(8,128)S(1)} %copy-done, f32[4096]{0:T(1024)S(1)} %broadcast_multiply_fusion, f32[128,2048]{0,1:T(8,128)S(1)} %get-tuple-element.11), kind=kOutput, calls=%fused_computation.72 | convolution fusion | flops 3221749760 | bytes 10764288 | tf_op jit(solution)/shard_map/dot_general | solution.py:50
  486.2 7.4 %fusion.57 = f32[512,4096]{1,0:T(8,128)S(1)} fusion(f32[128,4096]{1,0:T(8,128)S(1)} %copy-done, f32[4096]{0:T(1024)S(1)} %broadcast_multiply_fusion, f32[128,2048]{0,1:T(8,128)S(1)} %get-tuple-element.11), kind=kOutput, calls=%fused_computation.70 | convolution fusion | flops 3221749760 | bytes 10764288 | tf_op jit(solution)/shard_map/dot_general | solution.py:50
  494.4 5.5 mul.237
  499.8 12.1 %fusion.4 = f32[128,4096]{1,0:T(8,128)S(1)} fusion(f32[64,8,32,128]{3,2,1,0:T(8,128)} %bitcast.96, f32[512,4096]{1,0:T(8,128)} %fusion.61, f32[512]{0:T(512)S(1)} %get-tuple-element.36, f32[128,2048]{0,1:T(8,128)S(1)} %multiply_add_fusion), kind=kOutput, calls=%fused_computation.9 | convolution fusion | flops 3227516928 | bytes 19138560 | tf_op jit(solution)/shard_map/dot_general | solution.py:61
  512.0 5.7 mul.234
  517.6 12.3 %fusion.35 = f32[128,4096]{1,0:T(8,128)S(1)} fusion(f32[128,4096]{1,0:T(8,128)S(1)} %fusion.4, f32[64,8,32,128]{3,2,1,0:T(8,128)} %bitcast.93, f32[512,4096]{1,0:T(8,128)} %fusion.63, f32[512]{0:T(512)S(1)} %get-tuple-element.37, f32[128,2048]{0,1:T(8,128)S(1)} %multiply_add_fusion), kind=kOutput, calls=%fused_computation.45 | convolution fusion | flops 3228041216 | bytes 21235712 | tf_op jit(solution)/shard_map/dot_general | solution.py:61
  530.0 5.7 mul.240
  535.6 14.7 %fusion.36 = f32[128,4096]{1,0:T(8,128)} fusion(f32[128,4096]{1,0:T(8,128)S(1)} %fusion.35, f32[64,8,32,128]{3,2,1,0:T(8,128)} %bitcast.94, f32[512,4096]{1,0:T(8,128)S(1)} %fusion.59, f32[512]{0:T(512)S(1)} %get-tuple-element.35, f32[128,2048]{0,1:T(8,128)S(1)} %multiply_add_fusion), kind=kOutput, calls=%fused_computation.46 | convolution fusion | flops 3228041216 | bytes 21235712 | tf_op jit(solution)/shard_map/dot_general | solution.py:61
  550.4 2.5 mul.243
  552.9 11.6 %fusion.39 = f32[128,1,4096]{2,0,1:T(8,128)S(1)} fusion(f32[128,4096]{1,0:T(8,128)S(1)} %copy-done, f32[128,4096]{1,0:T(8,128)} %fusion.36, f32[64,8,32,128]{3,2,1,0:T(8,128)S(1)} %bitcast.90, f32[512,4096]{1,0:T(8,128)S(1)} %fusion.57, f32[512]{0:T(512)S(1)} %get-tuple-element.34, f32[128,2048]{0,1:T(8,128)S(1)} %multiply_add_fusion), kind=kOutput, calls=%fused_computation.49 | convolution fusion | flops 3228565504 | bytes 23332864 | tf_op jit(solution)/shard_map/dot_general | solution.py:61
  566.7 36.1 %all_to_all.32 = f32[128,1,4096]{2,1,0:T(1,128)S(1)} all-to-all(f32[128,1,4096]{2,1,0:T(1,128)S(1)} %copy.32), channel_id=1, replica_groups=mesh['gx'=8,'gy'=16] {'gx','gy'}, dimensions={0} | all-to-all | bytes 4194304 | tf_op jit(solution)/shard_map/all_to_all | solution.py:88
  (56 shorter events, 30.6 us)
Async XLA Ops:
  6.5 41.0 %all-to-all-start = ((f32[1,128,4096]{2,0,1:T(1,128)}), f32[1,128,4096]{2,0,1:T(1,128)S(1)}, u32[]{:S(2)}, u32[]{:S(2)}) async-start(f32[1,128,4096]{2,0,1:T(1,128)} %bitcast.98), calls=%async_computation | async-start | bytes 4194304 | tf_op jit(solution)/shard_map/all_to_all | solution.py:78
  18.0 187.5 %all-reduce.3.cloned.1.call-start = ((), (), s32[]{:S(2)}) async-start(), calls=%async_computation.2 | async-start | bytes 2097152 | tf_op jit(solution)/shard_map/psum | solution.py:82
  61.5 396.1 %all-reduce.5.cloned.1.call-start = ((), (), s32[]{:S(2)}) async-start(), calls=%async_computation.3 | async-start | bytes 2097152 | tf_op jit(solution)/shard_map/psum | solution.py:82
  302.6 7.4 %copy-start.1 = (f32[1,2048]{1,0:T(1,128)S(1)}, f32[1,2048]{1,0:T(1,128)}, u32[]{:S(2)}) copy-start(f32[1,2048]{1,0:T(1,128)} %get-tuple-element.30) | copy-start | bytes 24580
  302.6 7.4 %copy-start.4 = (pred[2048]{0:T(1024)(128)(4,1)S(1)}, pred[2048]{0:T(1024)(128)(4,1)}, u32[]{:S(2)}) copy-start(pred[2048]{0:T(1024)(128)(4,1)} %compare_and_fusion) | copy-start | bytes 6148
  310.0 151.1 %copy-start = (f32[128,4096]{1,0:T(8,128)S(1)}, f32[128,4096]{1,0:T(8,128)}, u32[]{:S(2)}) copy-start(f32[128,4096]{1,0:T(8,128)} %get-tuple-element.43) | copy-start | bytes 6291460
  486.2 7.4 %copy-start.2 = (f32[2,2048]{1,0:T(2,128)S(1)}, f32[2,2048]{1,0:T(2,128)}, u32[]{:S(2)}) copy-start(f32[2,2048]{1,0:T(2,128)} %param.13) | copy-start | bytes 49156
  486.2 7.4 %copy-start.3 = (f32[2,2048]{1,0:T(2,128)S(1)}, f32[2,2048]{1,0:T(2,128)}, u32[]{:S(2)}) copy-start(f32[2,2048]{1,0:T(2,128)} %param.14) | copy-start | bytes 49156
Sparse Core Ops, SparseCore 0:
  61.7 143.7 all-reduce.2
  311.7 145.9 all-reduce.4
where the time goes:
time: 615 us; the launch traced here: 611 us
  waiting for transfers between devices  307 us (50%)
  matrix products  165 us (27%)
  local copies, waits for them, and re-layouts  58.6 us (10%)
  blocking collectives  36.1 us (6%)
  other arithmetic  18.6 us (3%)
  between operations  14.1 us (2%)
  starting transfers between devices  12 us (2%)
    psum x2, waiting for transfers between devices, body(): priors = lax.psum(local_rows, ('gx', 'gy'))  285 us
    dot_general x8, matrix products, analyse(): jnp.dot(obs_shift[:, start:start + block_obs], localized, precision=lax.P...  102 us
    dot_general x8, matrix products, analyse(): jnp.dot(dev_part.T, state_dev, precision=lax.Precision.HIGHEST, preferred...  63 us
    all_to_all x1, blocking collectives, body(): lax.all_to_all(slabs, ('gx', 'gy'), split_axis=0, concat_axis=1, tiled=True)  36.1 us
    mul x8, local copies, waits for them, and re-layouts, analyse(): regress.reshape(block_obs, tiles_here, width // tiles_here)  29.9 us
    all_to_all x1, waiting for transfers between devices, body(): lax.all_to_all(ensemble, ('gx', 'gy'), split_axis=1, concat_axis=0, tiled...  21.9 us
    gather x2, local copies, waits for them, and re-layouts, body(): local_rows = jnp.take(slabs, obs_local[batch], axis=1) * owned[None, :]  13.5 us
  transfers between devices with their start and end apart: 3, of which 3 were waited for; matrix products, arithmetic and copies ran while one was open for 2% of the time, Pallas kernels for 0%

commit v1 on v0

--- a/solution.py
+++ b/solution.py
@@ -1,13 +1,27 @@
 import jax
 import jax.numpy as jnp
 from jax import lax
+from jax.experimental import pallas as pl
+from jax.experimental.pallas import tpu as pltpu
 from jax.sharding import PartitionSpec as P
 
 TILE = 128
 VAR_DEV = 4096
-
+TILES = VAR_DEV // TILE
+SLABS = 128
+MEMBERS = 128
+NOB = 2048
+AXES = ("gx", "gy")
+
+SLOTS = 64
+FAR_SLOTS = 32
+FAR_SLAB = SLABS // 2 - 1
+ROWS_OUT = TILES + 8
+CHUNK = 256
 
 epsilon = 1e-06
+F32 = jnp.float32
+BF16 = jnp.bfloat16
 
 
 def table_lookup(index_row, weight_table):
@@ -67,26 +81,336 @@
     return slab + total
 
 
+def general(ensemble, me, obs_owner, obs_local, obs_value, obs_errvar, tile_list, weight_index, weight_table):
+    slabs = lax.all_to_all(ensemble, AXES, split_axis=1, concat_axis=0, tiled=True)
+    for batch in range(2):
+        owned = (obs_owner[batch] == me).astype(jnp.float32)
+        local_rows = jnp.take(slabs, obs_local[batch], axis=1) * owned[None, :]
+        mine = lax.all_to_all(local_rows, AXES, split_axis=0, concat_axis=0, tiled=True)
+        mine = jnp.broadcast_to(jnp.sum(mine, axis=0), mine.shape)
+        priors = lax.all_to_all(mine, AXES, split_axis=0, concat_axis=0, tiled=True)
+        obs_dev, obs_spread, obs_shift = increments(priors, obs_value[batch], obs_errvar[batch])
+        weights = weights_for(
+            tile_list[batch], weight_index[batch], weight_table, me * TILES, TILES
+        )
+        slabs = analyse(slabs, obs_dev, obs_spread, obs_shift, weights)
+    return lax.all_to_all(slabs, AXES, split_axis=0, concat_axis=1, tiled=True)
+
+
+def dot_nt(a, b):
+    return lax.dot_general(a, b, (((1,), (1,)), ((), ())), preferred_element_type=F32)
+
+
+def dot_tn(a, b):
+    return lax.dot_general(a, b, (((0,), (0,)), ((), ())), preferred_element_type=F32)
+
+
+def dot_nn(a, b):
+    return lax.dot_general(a, b, (((1,), (0,)), ((), ())), preferred_element_type=F32)
+
+
+def split2(x):
+    hi = x.astype(BF16)
+    return hi, (x - hi.astype(F32)).astype(BF16)
+
+
+def split3(x):
+    hi = x.astype(BF16)
+    rest = x - hi.astype(F32)
+    mid = rest.astype(BF16)
+    return hi, mid, (rest - mid.astype(F32)).astype(BF16)
+
+
+def iota(shape, axis):
+    return lax.broadcasted_iota(jnp.int32, shape, axis)
+
+
+def send_kernel(tile_s, row_ref, lane_ref, owner_ref, out_ref, key_ref, flag_ref, buf, pad):
+    unroll = 16
+
+    def pick(i, carry):
+        base = pl.multiple_of(i * unroll, unroll)
+        for j in range(unroll):
+            buf[pl.ds(base + j, 1), :] = row_ref[pl.ds(tile_s[base + j], 1), :]
+        return carry
+
+    lax.fori_loop(0, 2 * NOB // unroll, pick, 0)
+
+    def copy(i, carry):
+        src = pl.multiple_of(i * TILES, 8)
+        dst = pl.multiple_of(i * ROWS_OUT, 8)
+        out_ref[pl.ds(dst, TILES), :] = row_ref[pl.ds(src, TILES), :]
+        return carry
+
+    lax.fori_loop(0, SLABS, copy, 0)
+
+    block = 512
+    sub128 = iota((128, 128), 0)
+    sub = iota((128, block), 0)
+    strict = (iota((block, block), 0) < iota((block, block), 1)).astype(F32).astype(BF16)
+    ones = jnp.ones((block, 128), BF16)
+    pad[...] = jnp.zeros_like(pad)
+    over = jnp.zeros((128, 128), F32)
+    for b in range(2):
+        count = jnp.zeros((128, 128), F32)
+        table = jnp.zeros((128, 128), F32)
+        for q in range(NOB // block):
+            own = owner_ref[b : b + 1, q * block : (q + 1) * block]
+            hit = own == sub
+            hit16 = hit.astype(F32).astype(BF16)
+            before = dot_nn(hit16, strict) + jnp.concatenate([count] * (block // 128), axis=1)
+            rank = jnp.sum(jnp.where(hit, before, 0.0), axis=0, keepdims=True).astype(jnp.int32)
+            key_ref[b : b + 1, q * block : (q + 1) * block] = own * SLOTS + rank
+            slot16 = (rank == (sub & (SLOTS - 1))).astype(F32).astype(BF16)
+            pieces = []
+            for k in range(block // 128):
+                at = b * (NOB // 128) + q * (block // 128) + k
+                part = buf[at * 128 : (at + 1) * 128, :].T
+                lane = lane_ref[at : at + 1, :]
+                pieces.append(jnp.sum(jnp.where(lane == sub128, part, 0.0), axis=0, keepdims=True))
+            picked = jnp.concatenate(pieces, axis=1)
+            for part in split3(jnp.where(hit, picked, 0.0)):
+                table = table + dot_nt(part, slot16)
+            count = count + dot_nn(hit16, ones)
+        limit = jnp.full((128, 128), float(SLOTS), F32)
+        if b == 0:
+            limit = jnp.where(sub128 >= SLABS - 3, float(FAR_SLOTS), limit)
+        over = jnp.maximum(over, jnp.where(count > limit, 1.0, 0.0))
+        pad[b, 8:136, :] = table
+    flag_ref[0, 0] = jnp.max(over).astype(jnp.int32)
+
+    low = iota((128, 128), 1) < SLOTS
+    for r in range(4):
+        out_ref[pl.ds(TILES + r, SLABS, stride=ROWS_OUT), :] = jnp.where(
+            low, pad[0, 4 + 2 * r : 132 + 2 * r, :], pad[0, 5 + 2 * r : 133 + 2 * r, :]
+        )
+    out_ref[pl.ds(TILES + 4, SLABS, stride=ROWS_OUT), :] = jnp.where(
+        low, pad[0, 12:140, :], pad[1, 6:134, :]
+    )
+    for r in range(2):
+        out_ref[pl.ds(TILES + 5 + r, SLABS, stride=ROWS_OUT), :] = jnp.where(
+            low, pad[1, 7 + 2 * r : 135 + 2 * r, :], pad[1, 8 + 2 * r : 136 + 2 * r, :]
+        )
+    lanes = iota((1, 128), 1)
+    far = jnp.where(
+        lanes < 32,
+        pad[0, 133:134, :],
+        jnp.where(
+            lanes < 64,
+            pltpu.roll(pad[0, 134:135, :], 32, 1),
+            jnp.where(lanes < 96, pad[0, 135:136, :], pltpu.roll(pad[1, 135:136, :], 32, 1)),
+        ),
+    )
+    out_ref[pl.ds(TILES + 7, SLABS, stride=ROWS_OUT), :] = jnp.broadcast_to(far, (128, 128))
+
+
+def send(ensemble, obs_owner, obs_local):
+    tile = (obs_owner * TILES + obs_local // TILE).reshape(2 * NOB)
+    lane = (obs_local % TILE).reshape(2 * NOB // 128, 128)
+    vmem = pl.BlockSpec(memory_space=pltpu.VMEM)
+    smem = pl.BlockSpec(memory_space=pltpu.SMEM)
+    return pl.pallas_call(
+        send_kernel,
+        out_shape=(
+            jax.ShapeDtypeStruct((SLABS * ROWS_OUT, 128), F32),
+            jax.ShapeDtypeStruct((2, NOB), jnp.int32),
+            jax.ShapeDtypeStruct((1, 1), jnp.int32),
+        ),
+        in_specs=[smem, vmem, vmem, vmem],
+        out_specs=(vmem, vmem, smem),
+        scratch_shapes=[pltpu.VMEM((2 * NOB, 128), F32), pltpu.VMEM((2, 144, 128), F32)],
+        compiler_params=pltpu.CompilerParams(vmem_limit_bytes=40 << 20),
+        cost_estimate=pl.CostEstimate(flops=10**9, bytes_accessed=5 << 20, transcendentals=0),
+        name="send",
+    )(tile, ensemble.reshape(VAR_DEV, 128), lane, obs_owner)
+
+
+def exact_dot(a, b, dims):
+    return lax.dot_general(
+        a, b, (dims, ((), ())), precision=lax.Precision.HIGHEST, preferred_element_type=F32
+    )
+
+
+def slot_keys(me):
+    def in_range(slab, rank, keep):
+        return jnp.where(keep & (slab >= 0) & (slab < SLABS), slab * SLOTS + rank, -1)
+
+    is_far = me == FAR_SLAB
+    j = jnp.arange(640, dtype=jnp.int32)
+    near0 = in_range(me - 4 + j // SLOTS, j % SLOTS, j < 576)
+    f = jnp.arange(128, dtype=jnp.int32)
+    reaches_far = jnp.abs(me - FAR_SLAB) <= 2
+    far0 = in_range(SLABS - 3 + f // FAR_SLOTS, f % FAR_SLOTS, (f < 96) & reaches_far)
+    i = jnp.arange(384, dtype=jnp.int32) - SLOTS
+    near1 = in_range(me - 2 + i // SLOTS, i % SLOTS, i >= 0)
+    far1 = in_range(jnp.full((128,), SLABS - 1, jnp.int32), f - 96, (f >= 96) & is_far)
+    return jnp.concatenate([near0, far0]), jnp.concatenate([near1, far1])
+
+
+def compaction(weights):
+    touch = jnp.any(weights != 0.0, axis=1)
+    place = jnp.cumsum(touch.astype(jnp.int32))
+    count = place[-1]
+    return jnp.where(touch, place - 1, -1), (count + CHUNK - 1) // CHUNK
+
+
+def tables(me, key, obs_owner, obs_local, obs_value, obs_errvar, tile_list, weight_index, weight_table):
+    keys = slot_keys(me)
+    cols, rows = [], []
+    for b in range(2):
+        select = (keys[b][:, None] == key[b][None, :]).astype(F32)
+        table_pick = jnp.where(tile_list[b] >= 0, table_lookup(weight_index[b], weight_table), 0.0)
+        per_obs = jnp.concatenate([tile_list[b].astype(F32), table_pick], axis=1)
+        cols.append(exact_dot(select, per_obs, ((1,), (0,))))
+        own_tile = (obs_owner[b] * TILES + obs_local[b] // TILE).astype(F32)
+        lines = jnp.stack([obs_value[b], obs_errvar[b], jnp.ones((NOB,), F32), own_tile])
+        rows.append(exact_dot(lines, select, ((1,), (1,))))
+    near = (me - 2) * TILES + jnp.arange(5 * TILES, dtype=jnp.int32)
+    far = jnp.where(me == FAR_SLAB, (SLABS - 1) * TILES + jnp.arange(TILES, dtype=jnp.int32), -2)
+    tile_ids = jnp.concatenate([near, far]).astype(F32)
+
+    def on_tiles(col, ids):
+        hit = col[:, :8, None] == ids[None, None, :]
+        return jnp.sum(jnp.where(hit, col[:, 8:, None], 0.0), axis=1)
+
+    spread0 = on_tiles(cols[0], tile_ids)
+    weights0 = spread0[:, 2 * TILES : 3 * TILES]
+    weights1 = on_tiles(cols[1], tile_ids[2 * TILES : 3 * TILES])
+    meet = (rows[1][3][None, :] == tile_ids[:, None]).astype(F32)
+    cross = exact_dot(spread0, meet, ((1,), (0,)))
+    place0, chunks0 = compaction(weights0)
+    place1, chunks1 = compaction(weights1)
+    out = []
+    for row, place, weights in ((rows[0], place0, weights0), (rows[1], place1, weights1)):
+        occupied = row[2]
+        lines = jnp.stack([row[0], row[1] + (1.0 - occupied), place.astype(F32)])
+        lines = jnp.concatenate([lines, jnp.zeros((5, lines.shape[1]), F32)])
+        out.append((lines, weights.T))
+    return jnp.stack([chunks0, chunks1]), cross, out[0], out[1]
+
+
+def obs_stats(priors, lines):
+    value, errvar = lines[0:1, :], lines[1:2, :]
+    mean = jnp.mean(priors, axis=0, keepdims=True)
+    dev = priors - mean
+    spread = jnp.sum(dev * dev, axis=0, keepdims=True) / (MEMBERS - 1.0)
+    denominator = spread + errvar
+    post_mean = (errvar * mean + spread * value) / denominator
+    shift = post_mean - mean + (jnp.sqrt(errvar / denominator) - 1.0) * dev
+    scale = 1.0 / ((MEMBERS - 1.0) * (spread + epsilon))
+    return dev, shift * scale
+
+
+def analyse_kernel(
+    chunks_s, r_ref, cross_ref, lines0_ref, w0_ref, lines1_ref, w1_ref, out_ref, acc_ref
+):
+    def payload(r):
+        return r_ref[pl.ds(TILES + r, MEMBERS, stride=ROWS_OUT), :]
+
+    def factors(b, dev, gain, lines, w_ref):
+        width = dev.shape[1]
+        dev_parts = split2(dev)
+        gain_parts = split2(gain)
+        place = lines[2:3, :].astype(jnp.int32)
+
+        def chunk(c, carry):
+            pick = (place == iota((CHUNK, width), 0) + c * CHUNK).astype(F32).astype(BF16)
+            dev_hi, dev_lo = [dot_nt(p, pick).astype(BF16) for p in dev_parts]
+            gain_c = dot_nt(gain_parts[0], pick) + dot_nt(gain_parts[1], pick)
+            dev_both = jnp.concatenate([dev_hi, dev_lo], axis=0)
+            w_here = dot_nt(split3(w_ref[...])[0], pick)
+            for part in split3(w_ref[...])[1:]:
+                w_here = w_here + dot_nt(part, pick)
+
+            for t in range(TILES):
+                lhs_hi, lhs_lo = split2(gain_c * w_here[t : t + 1, :])
+                both = dot_nt(lhs_hi, dev_both) + dot_nt(lhs_lo, dev_both)
+                a = both[:, :128] + both[:, 128:]
+
+                @pl.when(c == 0)
+                def _():
+                    acc_ref[b, t] = a
+
+                @pl.when(c > 0)
+                def _():
+                    acc_ref[b, t] = acc_ref[b, t] + a
+
+            return carry
+
+        lax.fori_loop(0, jnp.maximum(chunks_s[b], 1), chunk, 0)
+
+    part_rows = [payload(r) for r in range(8)]
+    priors0 = jnp.concatenate([part_rows[r] for r in (0, 1, 2, 3, 4, 7)], axis=1)
+    priors1 = jnp.concatenate([part_rows[r] for r in (4, 5, 6, 7)], axis=1)
+    dev0, gain0 = obs_stats(priors0, lines0_ref)
+
+    dev_hi, dev_lo = split2(dev0)
+    z_dev = priors1 - jnp.mean(priors1, axis=0, keepdims=True)
+    z_hi, z_lo = split2(z_dev)
+    covariance = dot_tn(
+        jnp.concatenate([dev_hi, dev_lo], axis=0), jnp.concatenate([z_hi, z_hi], axis=0)
+    ) + dot_tn(dev_hi, z_lo)
+    c_hi, c_lo = split2(covariance * cross_ref[...])
+    g_hi, g_lo = split2(gain0)
+    priors1 = priors1 + (dot_nn(g_hi, c_hi) + dot_nn(g_lo, c_hi) + dot_nn(g_hi, c_lo))
+    dev1, gain1 = obs_stats(priors1, lines1_ref)
+
+    factors(0, dev0, gain0, lines0_ref, w0_ref)
+    factors(1, dev1, gain1, lines1_ref, w1_ref)
+
+    def update(b, t, x):
+        dev = x - jnp.mean(x, axis=0, keepdims=True)
+        hi, lo = split2(dev)
+        both = jnp.concatenate([hi, lo], axis=1)
+        a_hi, a_lo = split2(acc_ref[b, t])
+        step = dot_nn(jnp.concatenate([a_hi, a_lo], axis=1), jnp.concatenate([both, both], axis=0))
+        return x + (step[:, :128] + step[:, 128:])
+
+    for t in range(TILES):
+        x = r_ref[pl.ds(t, MEMBERS, stride=ROWS_OUT), :]
+        x = update(0, t, x)
+        x = update(1, t, x)
+        out_ref[pl.ds(t, MEMBERS, stride=TILES), :] = x
+
+
+def analyse_slab(received, chunks, cross, obs0, obs1):
+    vmem = pl.BlockSpec(memory_space=pltpu.VMEM)
+    smem = pl.BlockSpec(memory_space=pltpu.SMEM)
+    return pl.pallas_call(
+        analyse_kernel,
+        out_shape=jax.ShapeDtypeStruct((MEMBERS * TILES, 128), F32),
+        in_specs=[smem] + [vmem] * 6,
+        out_specs=vmem,
+        scratch_shapes=[pltpu.VMEM((2, TILES, MEMBERS, MEMBERS), F32)],
+        compiler_params=pltpu.CompilerParams(vmem_limit_bytes=48 << 20),
+        cost_estimate=pl.CostEstimate(flops=4 * 10**9, bytes_accessed=8 << 20, transcendentals=0),
+        name="analyse",
+    )(chunks, received, cross, obs0[0], obs0[1], obs1[0], obs1[1])
+
+
 def body(
     ensemble, obs_owner, obs_local, obs_value, obs_errvar, tile_list, weight_index, weight_table
 ):
-    count_gy = lax.axis_size("gy")
-    my_index = lax.axis_index("gx") * count_gy + lax.axis_index("gy")
-    tiles_slab = VAR_DEV // TILE
-    batches = obs_owner.shape[0]
-    early_list = []
-    slabs = lax.all_to_all(ensemble, ("gx", "gy"), split_axis=1, concat_axis=0, tiled=True)
-    for batch in range(batches):
-        owned = (obs_owner[batch] == my_index).astype(jnp.float32)
-        local_rows = jnp.take(slabs, obs_local[batch], axis=1) * owned[None, :]
-        priors = lax.psum(local_rows, ("gx", "gy"))
-        obs_dev, obs_spread, obs_shift = increments(priors, obs_value[batch], obs_errvar[batch])
-        weights = weights_for(
-            tile_list[batch], weight_index[batch], weight_table, my_index * tiles_slab, tiles_slab
-        )
-        slabs = analyse(slabs, obs_dev, obs_spread, obs_shift, weights)
-    result = lax.all_to_all(slabs, ("gx", "gy"), split_axis=0, concat_axis=1, tiled=True)
-    return result
+    me = lax.axis_index("gx") * lax.axis_size("gy") + lax.axis_index("gy")
+    obs = (obs_owner, obs_local, obs_value, obs_errvar, tile_list, weight_index, weight_table)
+    outgoing, key, flag = send(ensemble, obs_owner, obs_local)
+
+    received = lax.all_to_all(
+        outgoing.reshape(SLABS, ROWS_OUT, 128), AXES, split_axis=0, concat_axis=0, tiled=True
+    ).reshape(MEMBERS * ROWS_OUT, 128)
+    chunks, cross, obs0, obs1 = tables(me, key, *obs)
+    updated = analyse_slab(received, chunks, cross, obs0, obs1)
+    result = lax.all_to_all(
+        updated.reshape(MEMBERS, TILES, 128), AXES, split_axis=0, concat_axis=0, tiled=True
+    ).reshape(ensemble.shape)
+
+    def overflows(state):
+        return state[0] > 0
+
+    def redo(state):
+        return jnp.int32(0), general(ensemble, me, *obs)
+
+    return lax.while_loop(overflows, redo, (flag[0, 0], result))[1]
 
 
 def solution(mesh):

time: 615 us -> 138 us (0.22)
  waiting for transfers between devices: 307 us -> 28.7 us
  matrix products: 165 us -> 10.2 us
  local copies, waits for them, and re-layouts: 58.6 us -> 6.57 us
  Pallas kernels: 0 us -> 37.9 us
  other arithmetic: 18.6 us -> 4.98 us
  between operations: 14.1 us -> 1.63 us
    psum x2 -> x0, waiting for transfers between devices: 285 us -> none  [body(): priors = lax.psum(local_rows, ('gx', 'gy'))]
    dot_general x16 -> x5, matrix products: 165 us -> 10.2 us  [exact_dot(): lax.dot_general(a, b, (dims, ((), ())), precision=lax.Precision.HIGHEST,...]
    pallas_call x0 -> x2, Pallas kernels: none -> 37.9 us  [the longest x1 27 us: analyse_slab(): pl.pallas_call(analyse_kernel, out_shape=jax.ShapeDtypeStruct((MEMBERS *...]
    mul x8 -> x0, local copies, waits for them, and re-layouts: 29.9 us -> none  [analyse(): regress.reshape(block_obs, tiles_here, width // tiles_here)]
    gather x2 -> x0, local copies, waits for them, and re-layouts: 13.5 us -> none  [body(): local_rows = jnp.take(slabs, obs_local[batch], axis=1) * owned[None, :]]
    reduce_sum x6 -> x2, other arithmetic: 8.53 us -> 0.65 us  [on_tiles(): return jnp.sum(jnp.where(hit, col[:, 8:, None], 0.0), axis=1)]
    all_to_all x1, waiting for transfers between devices: 21.9 us -> 28.7 us  [body(): lax.all_to_all(outgoing.reshape(SLABS, ROWS_OUT, 128), AXES, split_axis=0...]
  transfers between devices with their start and end apart: 3 -> 1, of which waited for: 3 -> 1; matrix products, arithmetic and copies ran while one was open for 2% -> 4% of each run, Pallas kernels for 0% -> 0%
where the time goes in v1:
time: 138 us; the launch traced here: 137 us
  Pallas kernels  37.9 us (27%)
  blocking collectives  34.3 us (25%)
  waiting for transfers between devices  28.7 us (21%)
  starting transfers between devices  11.9 us (9%)
  matrix products  10.2 us (7%)
  local copies, waits for them, and re-layouts  6.57 us (5%)
  other arithmetic  4.98 us (4%)
  between operations  1.63 us (1%)
    all_to_all x1, blocking collectives, body(): lax.all_to_all(updated.reshape(MEMBERS, TILES, 128), AXES, split_axis=0,...  34.3 us
    all_to_all x1, waiting for transfers between devices, body(): lax.all_to_all(outgoing.reshape(SLABS, ROWS_OUT, 128), AXES, split_axis=0...  28.7 us
    pallas_call x1, Pallas kernels, analyse_slab(): pl.pallas_call(analyse_kernel, out_shape=jax.ShapeDtypeStruct((MEMBERS *...  27 us
    all_to_all x1, starting transfers between devices, body(): lax.all_to_all(outgoing.reshape(SLABS, ROWS_OUT, 128), AXES, split_axis=0...  11.9 us
    pallas_call x1, Pallas kernels, send(): pl.pallas_call(send_kernel, out_shape=(jax.ShapeDtypeStruct((SLABS * ROWS...  10.9 us
    dot_general x5, matrix products, exact_dot(): lax.dot_general(a, b, (dims, ((), ())), precision=lax.Precision.HIGHEST,...  10.2 us
    unnamed x12, local copies, waits for them, and re-layouts  3.81 us
  transfers between devices with their start and end apart: 1, of which 1 were waited for; matrix products, arithmetic and copies ran while one was open for 4% of the time, Pallas kernels for 0%

profile of v1, /device:TPU:1, one launch (start us, length us, event | category | flops | bytes accessed | tf_op | source)
XLA Modules:
  0.0 137.1 jit_solution(16840846929135544)
XLA Ops:
  0.0 0.8 and_select_fusion.2
  0.9 10.9 %send.1 = (f32[5120,128]{1,0:T(8,128)}, s32[2,2048]{1,0:T(2,128)S(1)}, s32[1,1]{1,0:T(1,128)}) custom-call(s32[4096]{0:T(1024)S(1)} %bitcast.151, f32[4096,128]{1,0:T(8,128)} %bitcast.161, s32[32,128]{1,0:T(8,128)S(1)} %reshape.291.lane_ref, s32[2,2048]{1,0:T(2,128)} %owner_ref.1), custom_call_target="tpu_custom_call" | custom-call | flops 1000000000 | bytes 5242880 | tf_op jit(solution)/shard_map/send/pallas_call | solution.py:212
  11.8 0.9 slice_bitcast_fusion.5
  12.7 0.9 convert_bitcast_fusion.1
  13.6 1.2 select_reduce_fusion.6
  14.9 1.9 %fusion.111 = f32[512,16]{0,1:T(8,128)S(1)} fusion(s32[2048]{0:T(1024)S(1)} %bitcast.183, s32[512]{0:T(512)S(1)} %pad_add_fusion.1, f32[2048,8]{0,1:T(8,128)S(1)} %get-tuple-element.137, f32[2048,8]{0,1:T(8,128)S(1)} %get-tuple-element.135), kind=kOutput, calls=%fused_computation.165 | convolution fusion | flops 202407936 | bytes 174080 | tf_op jit(solution)/shard_map/dot_general | solution.py:229
  16.8 0.1 add_convert_fusion.2
  16.9 0.1 select_reduce_fusion.7
  17.1 0.3 reduce-window.24
  17.5 0.1 slice_reduce_fusion.1
  17.6 0.1 add_add_fusion
  17.7 0.6 slice.252
  19.0 2.7 %fusion.107 = f32[768,16]{0,1:T(8,128)S(1)} fusion(s32[2048]{0:T(1024)S(1)} %bitcast.181, s32[768]{0:T(1024)S(1)} %pad_add_fusion, f32[2048,8]{0,1:T(8,128)S(1)} %get-tuple-element.136, f32[2048,8]{0,1:T(8,128)S(1)} %get-tuple-element.134), kind=kOutput, calls=%fused_computation.161 | convolution fusion | flops 303595520 | bytes 191488 | tf_op jit(solution)/shard_map/dot_general | solution.py:229
  21.8 0.5 select_reduce_fusion.4
  22.3 0.3 reduce-window.16
  22.6 0.1 slice.241
  22.7 0.1 slice_reduce_fusion
  22.8 0.1 add_bitcast_fusion
  22.9 0.6 slice.243
  24.2 0.1 add_convert_fusion
  24.3 0.1 pad.14.clone
  24.4 0.1 pad.7.clone
  24.5 11.9 %all-to-all-start.6 = ((f32[128,40,128]{2,1,0:T(8,128)}), f32[128,40,128]{2,1,0:T(8,128)}, u32[]{:S(2)}, u32[]{:S(2)}) async-start(f32[128,40,128]{2,1,0:T(8,128)} %bitcast.41), calls=%async_computation.6 | async-start | bytes 5242880 | tf_op jit(solution)/shard_map/all_to_all | solution.py:398
  36.4 0.1 pad_add_fusion.2.chunks_s
  36.5 1.9 %fusion.109 = f32[4,512]{1,0:T(4,128)S(1)} fusion(s32[2048]{0:T(1024)S(1)} %bitcast.184, s32[512]{0:T(512)S(1)} %pad_add_fusion.1, f32[1,2048]{1,0:T(1,128)S(1)} %get-tuple-element.143, f32[1,2048]{1,0:T(1,128)S(1)} %get-tuple-element.163, f32[1,2048]{1,0:T(1,128)S(1)} %get-tuple-element.147, f32[4]{0:T(128)S(1)} %pad.14.clone), kind=kOutput, calls=%fused_computation.163 | convolution fusion | flops 51404800 | bytes 43024 | tf_op jit(solution)/shard_map/dot_general | solution.py:229
  38.5 2.7 %fusion.105 = f32[4,768]{1,0:T(4,128)S(1)} fusion(s32[2048]{0:T(1024)S(1)} %bitcast.182, s32[768]{0:T(1024)S(1)} %pad_add_fusion, f32[1,2048]{1,0:T(1,128)S(1)} %get-tuple-element.142, f32[1,2048]{1,0:T(1,128)S(1)} %get-tuple-element.164, f32[1,2048]{1,0:T(1,128)S(1)} %get-tuple-element.146, f32[4]{0:T(128)S(1)} %pad.14.clone), kind=kOutput, calls=%fused_computation.159 | convolution fusion | flops 77094912 | bytes 48144 | tf_op jit(solution)/shard_map/dot_general | solution.py:229
  41.4 1.0 fusion.121.cross_ref
  42.4 28.7 %all-to-all-done.6 = f32[128,40,128]{2,1,0:T(8,128)} async-done(((f32[128,40,128]{2,1,0:T(8,128)}), f32[128,40,128]{2,1,0:T(8,128)}, u32[]{:S(2)}, u32[]{:S(2)}) %all-to-all-start.6) | async-done | bytes 2621472 | tf_op jit(solution)/shard_map/all_to_all | solution.py:398
  71.0 27.0 %analyse.1 = f32[4096,128]{1,0:T(8,128)S(1)} custom-call(s32[2]{0:T(128)S(1)} %pad_add_fusion.2.chunks_s, f32[5120,128]{1,0:T(8,128)} %bitcast.42.r_ref, f32[768,512]{1,0:T(8,128)S(1)} %fusion.121.cross_ref, f32[8,768]{1,0:T(8,128)S(1)} %maximum_maximum_fusion.lines0_ref, f32[32,768]{1,0:T(8,128)S(1)} %slice_bitcast_fusion.4.w0_ref, ...), custom_call_target="tpu_custom_call" | custom-call | flops 4000000000 | bytes 8388608 | tf_op jit(solution)/shard_map/analyse/pallas_call | solution.py:379
  98.0 34.3 %all_to_all.65 = f32[128,32,128]{2,1,0:T(8,128)} all-to-all(f32[128,32,128]{2,1,0:T(8,128)S(1)} %bitcast.149), channel_id=1, replica_groups=mesh['gx'=8,'gy'=16] {'gx','gy'}, dimensions={0} | all-to-all | bytes 4194304 | tf_op jit(solution)/shard_map/all_to_all | solution.py:403
  132.4 0.9 while.9
  133.3 3.8 %copy.164 = f32[1,524288]{1,0:T(1,128)} copy(f32[1,524288]{1,0:T(1,128)} %get-tuple-element.277) | data formatting | bytes 4194304
  (41 shorter events, 0.7 us)
Async XLA Ops:
  0.0 24.1 %copy-start.11 = (s32[2,2048]{1,0:T(2,128)S(1)}, s32[2,2048]{1,0:T(2,128)}, u32[]{:S(2)}) copy-start(s32[2,2048]{1,0:T(2,128)} %param.14) | copy-start | bytes 49156
  0.0 24.2 %copy-start.13 = (s32[2,2048]{1,0:T(2,128)S(1)}, s32[2,2048]{1,0:T(2,128)}, u32[]{:S(2)}) copy-start(s32[2,2048]{1,0:T(2,128)} %owner_ref.1) | copy-start | bytes 49156
  0.0 14.8 %copy-start.9 = (s32[2,2048,8]{1,2,0:T(8,128)S(1)}, s32[2,2048,8]{1,2,0:T(8,128)}, u32[]{:S(2)}) copy-start(s32[2,2048,8]{1,2,0:T(8,128)} %param.17) | copy-start | bytes 393220
  14.8 21.6 %copy-start.15 = (f32[2,2048]{1,0:T(2,128)S(1)}, f32[2,2048]{1,0:T(2,128)}, u32[]{:S(2)}) copy-start(f32[2,2048]{1,0:T(2,128)} %param.15) | copy-start | bytes 49156
  14.9 21.6 %copy-start.17 = (f32[2,2048]{1,0:T(2,128)S(1)}, f32[2,2048]{1,0:T(2,128)}, u32[]{:S(2)}) copy-start(f32[2,2048]{1,0:T(2,128)} %param.16) | copy-start | bytes 49156
  24.5 46.6 %all-to-all-start.6 = ((f32[128,40,128]{2,1,0:T(8,128)}), f32[128,40,128]{2,1,0:T(8,128)}, u32[]{:S(2)}, u32[]{:S(2)}) async-start(f32[128,40,128]{2,1,0:T(8,128)} %bitcast.41), calls=%async_computation.6 | async-start | bytes 5242880 | tf_op jit(solution)/shard_map/all_to_all | solution.py:398

commit v2 on v1

v2 whole, which is shorter than its diff:
```python
import jax
import jax.numpy as jnp
from jax import lax
from jax.experimental import pallas as pl
from jax.experimental.pallas import tpu as pltpu
from jax.sharding import PartitionSpec as P

TILE = 128
VAR_DEV = 4096
TILES = VAR_DEV // TILE
SLABS = 128
MEMBERS = 128
NOB = 2048
AXES = ("gx", "gy")

SLOTS = 64
FAR_SLOTS = 32
FAR_SLAB = SLABS // 2 - 1
ROWS_OUT = TILES + 8
CHUNK = 256
GROUP = 4

epsilon = 1e-06
F32 = jnp.float32
BF16 = jnp.bfloat16


def table_lookup(index_row, weight_table):
    table_ids = jnp.arange(weight_table.shape[0], dtype=jnp.int32)
    return jnp.sum(
        (index_row[:, :, None] == table_ids[None, None, :]).astype(jnp.float32)
        * weight_table[None, None, :],
        axis=2,
    )


def weights_for(tiles_row, index_row, weight_table, first_tile, count):
    tile_ids = first_tile + jnp.arange(count, dtype=jnp.int32)
    tile_hit = (tiles_row[:, :, None] == tile_ids[None, None, :]).astype(jnp.float32)
    table_pick = table_lookup(index_row, weight_table)
    return jnp.sum(tile_hit * table_pick[:, :, None], axis=1)


def increments(priors, value_row, errvar_row):
    members = priors.shape[0]
    obs_mean = jnp.mean(priors, axis=0)
    obs_dev = priors - obs_mean
    obs_spread = jnp.sum(obs_dev * obs_dev, axis=0) / (members - 1.0)
    denominator = obs_spread + errvar_row
    post_mean = (errvar_row * obs_mean + obs_spread * value_row) / denominator
    obs_shift = post_mean - obs_mean + (jnp.sqrt(errvar_row / denominator) - 1.0) * obs_dev
    return (obs_dev, obs_spread, obs_shift)


def analyse(slab, obs_dev, obs_spread, obs_shift, weights):
    members, width = slab.shape
    count_obs = obs_dev.shape[1]
    block_obs = min(512, count_obs)
    tiles_here = weights.shape[1]
    state_mean = jnp.mean(slab, axis=0)
    state_dev = slab - state_mean
    total = jnp.zeros_like(slab)
    for start in range(0, count_obs, block_obs):
        dev_part = obs_dev[:, start : start + block_obs]
        covariance = jnp.dot(
            dev_part.T,
            state_dev,
            precision=lax.Precision.HIGHEST,
            preferred_element_type=jnp.float32,
        ) / (members - 1.0)
        regress = covariance / (obs_spread[start : start + block_obs] + epsilon)[:, None]
        localized = (
            regress.reshape(block_obs, tiles_here, width // tiles_here)
            * weights[start : start + block_obs, :, None]
        ).reshape(block_obs, width)
        total = total + jnp.dot(
            obs_shift[:, start : start + block_obs],
            localized,
            precision=lax.Precision.HIGHEST,
            preferred_element_type=jnp.float32,
        )
    return slab + total


def general(slabs, me, obs_owner, obs_local, obs_value, obs_errvar, tile_list, weight_index, weight_table):
    for batch in range(2):
        owned = (obs_owner[batch] == me).astype(jnp.float32)
        local_rows = jnp.take(slabs, obs_local[batch], axis=1) * owned[None, :]
        mine = lax.all_to_all(local_rows, AXES, split_axis=0, concat_axis=0, tiled=True)
        mine = jnp.broadcast_to(jnp.sum(mine, axis=0), mine.shape)
        priors = lax.all_to_all(mine, AXES, split_axis=0, concat_axis=0, tiled=True)
        obs_dev, obs_spread, obs_shift = increments(priors, obs_value[batch], obs_errvar[batch])
        weights = weights_for(
            tile_list[batch], weight_index[batch], weight_table, me * TILES, TILES
        )
        slabs = analyse(slabs, obs_dev, obs_spread, obs_shift, weights)
    return slabs


def dot_nt(a, b):
    return lax.dot_general(a, b, (((1,), (1,)), ((), ())), preferred_element_type=F32)


def dot_tn(a, b):
    return lax.dot_general(a, b, (((0,), (0,)), ((), ())), preferred_element_type=F32)


def dot_nn(a, b):
    return lax.dot_general(a, b, (((1,), (0,)), ((), ())), preferred_element_type=F32)


def split2(x):
    hi = x.astype(BF16)
    return hi, (x - hi.astype(F32)).astype(BF16)


def split3(x):
    hi = x.astype(BF16)
    rest = x - hi.astype(F32)
    mid = rest.astype(BF16)
    return hi, mid, (rest - mid.astype(F32)).astype(BF16)


def iota(shape, axis):
    return lax.broadcasted_iota(jnp.int32, shape, axis)


def send_kernel(
    x_ref, owner_ref, local_ref, out_ref, key_ref, flag_ref, row, buf, pad, pay, tile_v, tile_s0, tile_s1, sems
):
    unroll = 64
    block = 512
    lane_bits = TILE - 1
    load = pltpu.make_async_copy(x_ref, row, sems.at[0])
    load.start()
    tile_v[...] = owner_ref[...] * TILES + lax.shift_right_logical(local_ref[...], 7)
    index0 = pltpu.make_async_copy(tile_v.at[0], tile_s0, sems.at[1])
    index1 = pltpu.make_async_copy(tile_v.at[1], tile_s1, sems.at[4])
    index0.start()
    index1.start()

    sub128 = iota((128, 128), 0)
    sub = iota((128, block), 0)
    strict = (iota((block, block), 0) < iota((block, block), 1)).astype(F32).astype(BF16)
    ones = jnp.ones((block, 128), BF16)
    pad[...] = jnp.zeros_like(pad)
    over = jnp.zeros((128, 128), F32)
    ranks = []
    for b in range(2):
        count = jnp.zeros((128, 128), F32)
        for q in range(NOB // block):
            own = owner_ref[b : b + 1, q * block : (q + 1) * block]
            hit = own == sub
            hit16 = hit.astype(F32).astype(BF16)
            before = dot_nn(hit16, strict) + jnp.concatenate([count] * (block // 128), axis=1)
            rank = jnp.sum(jnp.where(hit, before, 0.0), axis=0, keepdims=True).astype(jnp.int32)
            key_ref[b : b + 1, q * block : (q + 1) * block] = own * SLOTS + rank
            ranks.append(rank)
            count = count + dot_nn(hit16, ones)
        limit = jnp.full((128, 128), float(SLOTS), F32)
        if b == 0:
            limit = jnp.where(sub128 >= SLABS - 3, float(FAR_SLOTS), limit)
        over = jnp.maximum(over, jnp.where(count > limit, 1.0, 0.0))
    flag_ref[0, 0] = jnp.max(over).astype(jnp.int32)

    index0.wait()
    index1.wait()
    load.wait()
    slab = pltpu.make_async_copy(
        row.reshape(SLABS, TILES, 128), out_ref.at[:, 0:TILES, :], sems.at[2]
    )
    slab.start()

    for b, tile_s in enumerate((tile_s0, tile_s1)):

        def pick(i, carry, b=b, tile_s=tile_s):
            base = pl.multiple_of(i * unroll, unroll)
            for j in range(unroll):
                buf[pl.ds(b * NOB + base + j, 1), :] = row[pl.ds(tile_s[base + j], 1), :]
            return carry

        lax.fori_loop(0, NOB // unroll, pick, 0)

    for b in range(2):
        table = jnp.zeros((128, 128), F32)
        for q in range(NOB // block):
            own = owner_ref[b : b + 1, q * block : (q + 1) * block]
            hit = own == sub
            slot16 = (ranks[b * (NOB // block) + q] == (sub & (SLOTS - 1))).astype(F32).astype(BF16)
            pieces = []
            for k in range(block // 128):
                at = q * block + k * 128
                part = buf[b * NOB + at : b * NOB + at + 128, :].T
                lane = local_ref[b : b + 1, at : at + 128] & lane_bits
                pieces.append(jnp.sum(jnp.where(lane == sub128, part, 0.0), axis=0, keepdims=True))
            picked = jnp.concatenate(pieces, axis=1)
            for part in split3(jnp.where(hit, picked, 0.0)):
                table = table + dot_nt(part, slot16)
        pad[b, 8:136, :] = table

    low = iota((128, 128), 1) < SLOTS
    for r in range(4):
        pay[:, r, :] = jnp.where(
            low, pad[0, 4 + 2 * r : 132 + 2 * r, :], pad[0, 5 + 2 * r : 133 + 2 * r, :]
        )
    pay[:, 4, :] = jnp.where(low, pad[0, 12:140, :], pad[1, 6:134, :])
    for r in range(2):
        pay[:, 5 + r, :] = jnp.where(
            low, pad[1, 7 + 2 * r : 135 + 2 * r, :], pad[1, 8 + 2 * r : 136 + 2 * r, :]
        )
    lanes = iota((1, 128), 1)
    far = jnp.where(
        lanes < 32,
        pad[0, 133:134, :],
        jnp.where(
            lanes < 64,
            pltpu.roll(pad[0, 134:135, :], 32, 1),
            jnp.where(lanes < 96, pad[0, 135:136, :], pltpu.roll(pad[1, 135:136, :], 32, 1)),
        ),
    )
    pay[:, 7, :] = jnp.broadcast_to(far, (128, 128))
    window = pltpu.make_async_copy(pay, out_ref.at[:, TILES:ROWS_OUT, :], sems.at[3])
    window.start()
    slab.wait()
    window.wait()


def send(ensemble, obs_owner, obs_local):
    vmem = pl.BlockSpec(memory_space=pltpu.VMEM)
    smem = pl.BlockSpec(memory_space=pltpu.SMEM)
    hbm = pl.BlockSpec(memory_space=pl.ANY)
    return pl.pallas_call(
        send_kernel,
        out_shape=(
            jax.ShapeDtypeStruct((SLABS, ROWS_OUT, 128), F32),
            jax.ShapeDtypeStruct((2, NOB), jnp.int32),
            jax.ShapeDtypeStruct((1, 1), jnp.int32),
        ),
        in_specs=[hbm, vmem, vmem],
        out_specs=(hbm, vmem, smem),
        scratch_shapes=[
            pltpu.VMEM((VAR_DEV, 128), F32),
            pltpu.VMEM((2 * NOB, 128), F32),
            pltpu.VMEM((2, 144, 128), F32),
            pltpu.VMEM((SLABS, 8, 128), F32),
            pltpu.VMEM((2, NOB), jnp.int32),
            pltpu.SMEM((NOB,), jnp.int32),
            pltpu.SMEM((NOB,), jnp.int32),
            pltpu.SemaphoreType.DMA((5,)),
        ],
        compiler_params=pltpu.CompilerParams(vmem_limit_bytes=60 << 20),
        cost_estimate=pl.CostEstimate(flops=10**9, bytes_accessed=5 << 20, transcendentals=0),
        name="send",
    )(ensemble.reshape(VAR_DEV, 128), obs_owner, obs_local)


SLOTS0 = 768
SLOTS1 = 512
CROSS_TILES = 256


def tables_kernel(
    me_s,
    table_s,
    key_ref,
    owner_ref,
    local_ref,
    value_ref,
    errvar_ref,
    list_ref,
    index_ref,
    cross_ref,
    lines0_ref,
    w0_ref,
    lines1_ref,
    w1_ref,
    chunks_ref,
):
    me = me_s[0, 0]
    at_far = me == FAR_SLAB
    near_far = (me >= FAR_SLAB - 2) & (me <= FAR_SLAB + 2)

    def slot_key(slab, rank, keep):
        return jnp.where(keep & (slab >= 0) & (slab < SLABS), slab * SLOTS + rank, -1)

    j = iota((SLOTS0, 128), 0)
    f = j - 640
    near = slot_key(me - 4 + lax.shift_right_logical(j, 6), j & 63, j < 576)
    far = slot_key(SLABS - 3 + lax.shift_right_arithmetic(f, 5), f & 31, (f < 96) & near_far)
    keys0 = jnp.where(j < 640, near, far)
    j = iota((SLOTS1, 128), 0)
    f = j - 384
    near = slot_key(me - 3 + lax.shift_right_logical(j, 6), j & 63, j >= 64)
    far = slot_key(jnp.full_like(j, SLABS - 1), f - 96, (f >= 96) & at_far)
    keys1 = jnp.where(j < 384, near, far)

    def tile_id(shape):
        k = iota(shape, 0)
        near_id = (me - 2) * TILES + k
        far_id = jnp.where((k < 192) & at_far, (SLABS - 1) * TILES + k - 160, -2)
        return jnp.where(k < 160, jnp.where(near_id < 0, -2, near_id), far_id)

    def on_tiles(b, ids):
        total = jnp.zeros(ids.shape, F32)
        for k in range(8):
            entry = index_ref[b, k : k + 1, :]
            pick = jnp.zeros(entry.shape, F32)
            for n in range(16):
                pick = jnp.where(entry == n, table_s[n], pick)
            total = total + jnp.where(list_ref[b, k : k + 1, :] == ids, pick, 0.0)
        return total

    def exact_nt(a, b):
        return sum(dot_nt(part, b) for part in split3(a))

    ids = tile_id((CROSS_TILES, NOB))
    own_ids = me * TILES + iota((TILES, NOB), 0)
    for b, (keys, lines_ref, w_ref) in enumerate(
        ((keys0, lines0_ref, w0_ref), (keys1, lines1_ref, w1_ref))
    ):
        slots = keys.shape[0]
        select = jnp.concatenate(
            [
                (keys == key_ref[b : b + 1, c * 128 : (c + 1) * 128]).astype(F32).astype(BF16)
                for c in range(NOB // 128)
            ],
            axis=1,
        )
        own_tile = owner_ref[b : b + 1, :] * TILES + lax.shift_right_logical(local_ref[b : b + 1, :], 7)
        lines = jnp.concatenate(
            [
                value_ref[b : b + 1, :],
                errvar_ref[b : b + 1, :] - 1.0,
                own_tile.astype(F32) + 1.0,
                jnp.zeros((5, NOB), F32),
            ],
            axis=0,
        )
        lines = exact_nt(lines, select)
        weights = exact_nt(on_tiles(b, own_ids), select)
        touch = jnp.max(jnp.where(weights != 0.0, 1.0, 0.0), axis=0, keepdims=True)
        upto = (iota((slots, slots), 0) <= iota((slots, slots), 1)).astype(F32).astype(BF16)
        place = dot_nn(jnp.broadcast_to(touch, (8, slots)).astype(BF16), upto)[0:1, :]
        chunks_ref[b] = (jnp.max(place).astype(jnp.int32) + CHUNK - 1) // CHUNK
        w_ref[...] = weights
        lines_ref[...] = jnp.concatenate(
            [
                lines[0:1, :],
                lines[1:2, :] + 1.0,
                jnp.where(touch > 0.0, place - 1.0, -1.0),
                jnp.zeros((5, slots), F32),
            ],
            axis=0,
        )
        if b == 0:
            spread = on_tiles(0, ids)
            spread = [dot_nt(select, part).astype(BF16) for part in split3(spread)]
        else:
            own_row = lines[2:3, :].astype(jnp.int32) - 1
            meet = (own_row == tile_id((CROSS_TILES, slots))).astype(F32).astype(BF16)
            cross_ref[...] = sum(dot_nn(part, meet) for part in spread)


def tables(me, key, obs_owner, obs_local, obs_value, obs_errvar, tile_list, weight_index, weight_table):
    vmem = pl.BlockSpec(memory_space=pltpu.VMEM)
    smem = pl.BlockSpec(memory_space=pltpu.SMEM)
    cross, lines0, w0, lines1, w1, chunks = pl.pallas_call(
        tables_kernel,
        out_shape=(
            jax.ShapeDtypeStruct((SLOTS0, SLOTS1), F32),
            jax.ShapeDtypeStruct((8, SLOTS0), F32),
            jax.ShapeDtypeStruct((TILES, SLOTS0), F32),
            jax.ShapeDtypeStruct((8, SLOTS1), F32),
            jax.ShapeDtypeStruct((TILES, SLOTS1), F32),
            jax.ShapeDtypeStruct((2,), jnp.int32),
        ),
        in_specs=[smem, smem] + [vmem] * 7,
        out_specs=(vmem, vmem, vmem, vmem, vmem, smem),
        compiler_params=pltpu.CompilerParams(vmem_limit_bytes=28 << 20),
        cost_estimate=pl.CostEstimate(flops=10**6, bytes_accessed=10**6, transcendentals=0),
        name="tables",
    )(
        me.reshape(1, 1).astype(jnp.int32),
        weight_table,
        key,
        obs_owner,
        obs_local,
        obs_value,
        obs_errvar,
        jnp.transpose(tile_list, (0, 2, 1)),
        jnp.transpose(weight_index, (0, 2, 1)),
    )
    return chunks, cross, (lines0, w0), (lines1, w1)


def obs_stats(priors, lines):
    value, errvar = lines[0:1, :], lines[1:2, :]
    mean = jnp.mean(priors, axis=0, keepdims=True)
    dev = priors - mean
    spread = jnp.sum(dev * dev, axis=0, keepdims=True) / (MEMBERS - 1.0)
    denominator = spread + errvar
    post_mean = (errvar * mean + spread * value) / denominator
    shift = post_mean - mean + (jnp.sqrt(errvar / denominator) - 1.0) * dev
    scale = 1.0 / ((MEMBERS - 1.0) * (spread + epsilon))
    return dev, shift * scale


def analyse_kernel(
    chunks_s, r_ref, cross_ref, lines0_ref, w0_ref, lines1_ref, w1_ref, out_ref, acc_ref, x_ref, sems
):
    received = r_ref.reshape(MEMBERS * ROWS_OUT, 128)

    def tile(t):
        return received[pl.ds(t, MEMBERS, stride=ROWS_OUT), :]

    def payload(r):
        return tile(TILES + r)

    def pick_of(place, c):
        return (place == iota((CHUNK, place.shape[1]), 0) + c * CHUNK).astype(F32).astype(BF16)

    def weights_of(w_ref, pick):
        return sum(dot_nt(part, pick) for part in split3(w_ref[...]))

    early = []
    for lines_ref, w_ref in ((lines0_ref, w0_ref), (lines1_ref, w1_ref)):
        pick = pick_of(lines_ref[2:3, :].astype(jnp.int32), 0)
        early.append((pick, weights_of(w_ref, pick)))

    def factors(b, dev, gain, lines, w_ref):
        width = dev.shape[1]
        dev_parts = split2(dev)
        gain_parts = split2(gain)
        place = lines[2:3, :].astype(jnp.int32)

        def chunk(c, first):
            if first:
                pick, w_here = early[b]
            else:
                pick = pick_of(place, c)
                w_here = weights_of(w_ref, pick)
            dev_both = jnp.concatenate([dot_nt(pick, p).astype(BF16) for p in dev_parts], axis=1)
            gain_c = dot_nt(gain_parts[0], pick) + dot_nt(gain_parts[1], pick)
            for start in range(0, TILES, GROUP):
                lhs = []
                for t in range(start, start + GROUP):
                    lhs.extend(split2(gain_c * w_here[t : t + 1, :]))
                both = dot_nn(jnp.concatenate(lhs, axis=0), dev_both)
                both = both[:, :128] + both[:, 128:]
                for k in range(GROUP):
                    a = both[256 * k : 256 * k + 128, :] + both[256 * k + 128 : 256 * k + 256, :]
                    acc_ref[b, start + k] = a if first else acc_ref[b, start + k] + a

        def more(c, carry):
            chunk(c, False)
            return carry

        chunk(0, True)
        lax.fori_loop(1, chunks_s[b], more, 0)

    part_rows = [payload(r) for r in range(8)]
    priors0 = jnp.concatenate([part_rows[r] for r in (0, 1, 2, 3, 4, 7)], axis=1)
    priors1 = jnp.concatenate([part_rows[r] for r in (4, 5, 6, 7)], axis=1)
    dev0, gain0 = obs_stats(priors0, lines0_ref)

    dev_hi, dev_lo = split2(dev0)
    z_dev = priors1 - jnp.mean(priors1, axis=0, keepdims=True)
    z_hi, z_lo = split2(z_dev)
    covariance = dot_tn(
        jnp.concatenate([dev_hi, dev_lo], axis=0), jnp.concatenate([z_hi, z_hi], axis=0)
    ) + dot_tn(dev_hi, z_lo)
    c_hi, c_lo = split2(covariance * cross_ref[...])
    g_hi, g_lo = split2(gain0)
    priors1 = priors1 + (dot_nn(g_hi, c_hi) + dot_nn(g_lo, c_hi) + dot_nn(g_hi, c_lo))
    dev1, gain1 = obs_stats(priors1, lines1_ref)

    factors(0, dev0, gain0, lines0_ref, w0_ref)
    factors(1, dev1, gain1, lines1_ref, w1_ref)

    def update(b, t, x):
        dev = x - jnp.mean(x, axis=0, keepdims=True)
        hi, lo = split2(dev)
        both = jnp.concatenate([hi, lo], axis=1)
        a_hi, a_lo = split2(acc_ref[b, t])
        step = dot_nn(jnp.concatenate([a_hi, a_lo], axis=1), jnp.concatenate([both, both], axis=0))
        return x + (step[:, :128] + step[:, 128:])

    leave = []
    for start in range(0, TILES, 8):
        group = range(start, start + 8)
        for t in group:
            x_ref[t] = update(1, t, update(0, t, tile(t)))
        for t in group:
            copy = pltpu.make_async_copy(x_ref.at[t], out_ref.at[:, t, :], sems.at[t])
            copy.start()
            leave.append(copy)
    for copy in leave:
        copy.wait()


def analyse_slab(received, chunks, cross, obs0, obs1):
    vmem = pl.BlockSpec(memory_space=pltpu.VMEM)
    smem = pl.BlockSpec(memory_space=pltpu.SMEM)
    hbm = pl.BlockSpec(memory_space=pl.ANY)
    return pl.pallas_call(
        analyse_kernel,
        out_shape=jax.ShapeDtypeStruct((MEMBERS, TILES, 128), F32),
        in_specs=[smem] + [vmem] * 6,
        out_specs=hbm,
        scratch_shapes=[
            pltpu.VMEM((2, TILES, MEMBERS, MEMBERS), F32),
            pltpu.VMEM((TILES, MEMBERS, 128), F32),
            pltpu.SemaphoreType.DMA((TILES,)),
        ],
        compiler_params=pltpu.CompilerParams(vmem_limit_bytes=24 << 20),
        cost_estimate=pl.CostEstimate(flops=4 * 10**9, bytes_accessed=8 << 20, transcendentals=0),
        name="analyse",
    )(chunks, received, cross, obs0[0], obs0[1], obs1[0], obs1[1])


def body(
    ensemble, obs_owner, obs_local, obs_value, obs_errvar, tile_list, weight_index, weight_table
):
    me = lax.axis_index("gx") * lax.axis_size("gy") + lax.axis_index("gy")
    obs = (obs_owner, obs_local, obs_value, obs_errvar, tile_list, weight_index, weight_table)
    outgoing, key, flag = send(ensemble, obs_owner, obs_local)

    received = lax.all_to_all(outgoing, AXES, split_axis=0, concat_axis=0, tiled=True)
    chunks, cross, obs0, obs1 = tables(me, key, *obs)
    updated = analyse_slab(received, chunks, cross, obs0, obs1)

    def overflows(state):
        return state[0] > 0

    def redo(state):
        slabs = received[:, :TILES, :].reshape(MEMBERS, VAR_DEV)
        return jnp.int32(0), general(slabs, me, *obs).reshape(MEMBERS, TILES, 128)

    updated = lax.while_loop(overflows, redo, (flag[0, 0], updated))[1]
    result = lax.all_to_all(updated, AXES, split_axis=0, concat_axis=0, tiled=True)
    return result.reshape(ensemble.shape)


def solution(mesh):
    placed = (P(("gx", "gy"), None), P(), P(), P(), P(), P(), P(), P())
    return jax.shard_map(
        body, mesh=mesh, in_specs=placed, out_specs=P(("gx", "gy"), None), check_vma=False
    )
```

time: 138 us -> 104 us (0.75)
  waiting for transfers between devices: 28.7 us -> 17.3 us
  matrix products: 10.2 us -> 0 us
  other arithmetic: 4.98 us -> 0 us
  local copies, waits for them, and re-layouts: 6.57 us -> 2.06 us
  between operations: 1.63 us -> 0.13 us
    all_to_all x1, waiting for transfers between devices: 28.7 us -> 17.3 us  [body(): lax.all_to_all(outgoing, AXES, split_axis=0, concat_axis=0, tiled=True)]
    dot_general x5 -> x0, matrix products: 10.2 us -> none  [exact_dot(): lax.dot_general(a, b, (dims, ((), ())), precision=lax.Precision.HIGHEST,...]
    reduce_sum x3 -> x0, other arithmetic: 1.83 us -> none  [the longest x1 1.18 us: table_lookup(): jnp.sum((index_row[:, :, None] == table_ids[None, None, :]).astype(jnp.fl...]
    unnamed x12 -> x15, local copies, waits for them, and re-layouts: 3.81 us -> 2.06 us
    slice x8 -> x0, local copies, waits for them, and re-layouts: 1.39 us -> none  [the longest x2 1.18 us: compaction(): count = place[-1]]
    pallas_call x2 -> x3, Pallas kernels: 37.9 us -> 37.2 us  [the longest x1 16.4 us: tables(): pl.pallas_call(tables_kernel, out_shape=(jax.ShapeDtypeStruct((SLOTS0, SL...]
  transfers between devices with their start and end apart: 1 -> 1, of which waited for: 1 -> 1; matrix products, arithmetic and copies ran while one was open for 4% -> 0% of each run, Pallas kernels for 0% -> 16%
where the time goes in v2:
time: 104 us
  Pallas kernels  37.2 us (36%)
  blocking collectives  34.4 us (33%)
  waiting for transfers between devices  17.3 us (17%)
  starting transfers between devices  12.1 us (12%)
  local copies, waits for them, and re-layouts  2.06 us (2%)
    all_to_all x1, blocking collectives, body(): lax.all_to_all(updated, AXES, split_axis=0, concat_axis=0, tiled=True)  34.4 us
    all_to_all x1, waiting for transfers between devices, body(): lax.all_to_all(outgoing, AXES, split_axis=0, concat_axis=0, tiled=True)  17.3 us
    pallas_call x1, Pallas kernels, tables(): pl.pallas_call(tables_kernel, out_shape=(jax.ShapeDtypeStruct((SLOTS0, SL...  16.4 us
    all_to_all x1, starting transfers between devices, body(): lax.all_to_all(outgoing, AXES, split_axis=0, concat_axis=0, tiled=True)  12.1 us
    pallas_call x1, Pallas kernels, analyse_slab(): pl.pallas_call(analyse_kernel, out_shape=jax.ShapeDtypeStruct((MEMBERS, T...  11.2 us
    pallas_call x1, Pallas kernels, send(): pl.pallas_call(send_kernel, out_shape=(jax.ShapeDtypeStruct((SLABS, ROWS_...  9.56 us
  transfers between devices with their start and end apart: 1, of which 1 were waited for; matrix products, arithmetic and copies ran while one was open for 0% of the time, Pallas kernels for 16%

profile of v2, /device:TPU:1, one launch (start us, length us, event | category | flops | bytes accessed | tf_op | source)
XLA Modules:
  0.0 104.1 jit_solution(17153060265343750113)
XLA Ops:
  0.0 0.0 copy-start.13
  0.0 0.0 copy-start.15
  0.0 0.0 copy-start.22
  0.0 0.0 copy-start.17
  0.0 0.0 copy-start.19
  0.0 0.0 copy-start.9
  0.0 9.6 %send.1 = (f32[128,40,128]{2,1,0:T(8,128)}, s32[2,2048]{1,0:T(2,128)}, s32[1,1]{1,0:T(1,128)}) custom-call(f32[4096,128]{1,0:T(8,128)} %bitcast.151, s32[2,2048]{1,0:T(2,128)} %owner_ref.3, s32[2,2048]{1,0:T(2,128)} %local_ref.3), custom_call_target="tpu_custom_call" | custom-call | flops 1000000000 | bytes 5242880 | tf_op jit(solution)/shard_map/send/pallas_call | solution.py:232
  9.6 12.1 %all-to-all-start.4 = ((f32[128,40,128]{2,1,0:T(8,128)}), f32[128,40,128]{2,1,0:T(8,128)}, u32[]{:S(2)}, u32[]{:S(2)}) async-start(f32[128,40,128]{2,1,0:T(8,128)} %get-tuple-element.73), calls=%async_computation.4 | async-start | bytes 5242880 | tf_op jit(solution)/shard_map/all_to_all | solution.py:528
  21.7 0.0 copy-done.13
  21.7 0.0 copy-done.15
  21.7 0.0 copy-done.22
  21.7 0.0 copy-done.17
  21.7 0.0 copy-done.19
  21.8 0.0 copy-done.9
  21.8 0.0 copy-start
  21.8 0.7 copy-done
  22.5 16.4 %tables.1 = (f32[768,512]{1,0:T(8,128)S(1)}, f32[8,768]{1,0:T(8,128)S(1)}, f32[32,768]{1,0:T(8,128)S(1)}, f32[8,512]{1,0:T(8,128)S(1)}, f32[32,512]{1,0:T(8,128)S(1)}, /*index=5*/s32[2]{0:T(128)S(1)}) custom-call(s32[1,1]{1,0:T(1,128)} %bitcast.23.me_s, f32[16]{0:T(128)S(1)} %copy-done.22, s32[2,2048]{1,0:T(2,128)S(1)} %copy-done, s32[2,2048]{1,0:T(2,128)S(1)} %copy-done.13, ...), custom_call_target="tpu_custom_call" | custom-call | flops 1000000 | bytes 1000000 | tf_op jit(solution)/shard_map/tables/pallas_call | solution.py:367
  38.9 17.3 %all-to-all-done.4.r_ref = f32[128,40,128]{2,1,0:T(8,128)} async-done(((f32[128,40,128]{2,1,0:T(8,128)}), f32[128,40,128]{2,1,0:T(8,128)}, u32[]{:S(2)}, u32[]{:S(2)}) %all-to-all-start.4) | async-done | bytes 2621472 | tf_op jit(solution)/shard_map/all_to_all | solution.py:528
  56.2 11.2 %analyse.1 = f32[128,32,128]{2,1,0:T(8,128)} custom-call(s32[2]{0:T(128)S(1)} %get-tuple-element.72.chunks_s, f32[128,40,128]{2,1,0:T(8,128)} %all-to-all-done.4.r_ref, f32[768,512]{1,0:T(8,128)S(1)} %get-tuple-element.74.cross_ref, f32[8,768]{1,0:T(8,128)S(1)} %get-tuple-element.75.lines0_ref, f32[32,768]{1,0:T(8,128)S(1)} %get-tuple-element.76.w0_ref, ...), custom_call_target="tpu_custom_call" | custom-call | flops 4000000000 | bytes 8388608 | tf_op jit(solution)/shard_map/analyse/pallas_call | solution.py:505
  67.4 0.9 while.9
  68.3 34.4 %all_to_all.40 = f32[128,32,128]{2,1,0:T(8,128)S(1)} all-to-all(f32[128,32,128]{2,1,0:T(8,128)} %get-tuple-element.271), channel_id=1, replica_groups=mesh['gx'=8,'gy'=16] {'gx','gy'}, dimensions={0} | all-to-all | bytes 4194304 | tf_op jit(solution)/shard_map/all_to_all | solution.py:540
  102.7 1.3 %copy.144 = f32[1,524288]{1,0:T(1,128)} copy(f32[1,524288]{1,0:T(1,128)S(1)} %bitcast.134) | data formatting | bytes 4194304
Async XLA Ops:
  0.0 21.7 %copy-start.13 = (s32[2,2048]{1,0:T(2,128)S(1)}, s32[2,2048]{1,0:T(2,128)}, u32[]{:S(2)}) copy-start(s32[2,2048]{1,0:T(2,128)} %owner_ref.3) | copy-start | bytes 49156
  0.0 21.7 %copy-start.15 = (s32[2,2048]{1,0:T(2,128)S(1)}, s32[2,2048]{1,0:T(2,128)}, u32[]{:S(2)}) copy-start(s32[2,2048]{1,0:T(2,128)} %local_ref.3) | copy-start | bytes 49156
  0.0 21.7 %copy-start.22 = (f32[16]{0:T(128)S(1)}, f32[16]{0:T(128)}, u32[]{:S(2)}) copy-start(f32[16]{0:T(128)} %table_s.1) | copy-start | bytes 196
  0.0 21.7 %copy-start.17 = (f32[2,2048]{1,0:T(2,128)S(1)}, f32[2,2048]{1,0:T(2,128)}, u32[]{:S(2)}) copy-start(f32[2,2048]{1,0:T(2,128)} %value_ref.1) | copy-start | bytes 49156
  0.0 21.7 %copy-start.19 = (f32[2,2048]{1,0:T(2,128)S(1)}, f32[2,2048]{1,0:T(2,128)}, u32[]{:S(2)}) copy-start(f32[2,2048]{1,0:T(2,128)} %errvar_ref.1) | copy-start | bytes 49156
  0.0 21.7 %copy-start.9 = (s32[2,2048,8]{1,2,0:T(8,128)S(1)}, s32[2,2048,8]{1,2,0:T(8,128)}, u32[]{:S(2)}) copy-start(s32[2,2048,8]{1,2,0:T(8,128)} %param.17) | copy-start | bytes 393220
  9.6 46.6 %all-to-all-start.4 = ((f32[128,40,128]{2,1,0:T(8,128)}), f32[128,40,128]{2,1,0:T(8,128)}, u32[]{:S(2)}, u32[]{:S(2)}) async-start(f32[128,40,128]{2,1,0:T(8,128)} %get-tuple-element.73), calls=%async_computation.4 | async-start | bytes 5242880 | tf_op jit(solution)/shard_map/all_to_all | solution.py:528
  21.8 0.7 copy-start
